TPU v7x, 32 devices: a whole 2x2x4 slice. The times are simulated.
32 devices in a mesh: groups: 2 (over x), seq: 16 (over z, y, core).
Axes of the slice: x: 2, y: 2, z: 4, core: 2. Of those that a mesh axis runs over, the one named last changes fastest.
Arguments:
- inputs: bfloat16 [16384, 768], P(('groups', 'seq')), parts along dimension 0, may hold values from -6 to 6
- gates: bfloat16 [16384, 768], P(('groups', 'seq')), parts along dimension 0, may hold values from -6 to 6
- cotangent: bfloat16 [16384, 768], P(('groups', 'seq')), parts along dimension 0, may hold values from -6 to 6
- first_factor: bfloat16 [16, 512, 512], P('seq'), may hold values from -0.25 to 0.25
- second_factor: bfloat16 [512, 16, 16], P('seq'), may hold values from -1.5 to 1.5
- channel_gain: float32 [768], replicated, may hold values from 0.1 to 1.9
Outputs:
- layer_output: bfloat16 [16384, 768], P(('groups', 'seq')), parts along dimension 0
- grad_inputs: bfloat16 [16384, 768], P(('groups', 'seq')), parts along dimension 0
- grad_gates: bfloat16 [16384, 768], P(('groups', 'seq')), parts along dimension 0
- grad_first: bfloat16 [32, 512, 512], P(('groups', 'seq')), parts along dimension 0
- grad_second: bfloat16 [1024, 16, 16], P(('groups', 'seq')), parts along dimension 0
- gain_grad: float32 [1536], P('groups'), parts along dimension 0
There are 2 independent parts, one for each index of `groups`. A program takes and returns all parts, laid end to end along the dimension named above; an argument that names none is the same for every part. Nothing has to cross between parts.
All inputs are finite; a program needn't handle non-finite values.
Results may differ from a plain program's by a relative error of at most 0.0085.
Values may be sent and summed in bfloat16 or wider, within the bound.
A program may use at most 64 MiB of HBM per device.

v0:
```python
import math
import jax
import jax.numpy as jnp
from jax import lax
from jax.sharding import PartitionSpec as P


def lower_mask(extent):
    row_ids = lax.broadcasted_iota(jnp.int32, (extent, extent), 0)
    col_ids = lax.broadcasted_iota(jnp.int32, (extent, extent), 1)
    return col_ids <= row_ids


def on_device(inputs, gates, cotangent, first_factor, second_factor, channel_gain):
    block_count = first_factor.shape[0]
    block_size = first_factor.shape[1]
    channels = inputs.shape[1]
    block_total = second_factor.shape[1]
    rows3 = inputs.reshape(block_count, block_size, channels)
    gates3 = gates.reshape(block_count, block_size, channels)
    upstream3 = cotangent.reshape(block_count, block_size, channels)
    mask_first = lower_mask(block_size)
    mask_second = lower_mask(block_total)
    first_masked = jnp.where(mask_first[None], first_factor, jnp.zeros((), first_factor.dtype))
    second_masked = jnp.where(mask_second[None], second_factor, jnp.zeros((), second_factor.dtype))
    norm_factor = 1.0 / math.sqrt(inputs.shape[0] * lax.axis_size("seq"))
    gates_cols, upstream_cols = (
        lax.all_to_all(gates3, "seq", split_axis=1, concat_axis=0, tiled=True),
        lax.all_to_all(upstream3, "seq", split_axis=1, concat_axis=0, tiled=True),
    )
    first_mixed = jnp.einsum(
        "kab,kbc->kac", first_masked, rows3, preferred_element_type=jnp.float32
    ).astype(jnp.bfloat16)
    columns = lax.all_to_all(first_mixed, "seq", split_axis=1, concat_axis=0, tiled=True)
    second_cols = jnp.einsum(
        "jab,bjc->ajc", second_masked, columns, preferred_element_type=jnp.float32
    ).astype(jnp.bfloat16)
    hidden_values = second_cols.astype(jnp.float32)
    gate_values = gates_cols.astype(jnp.float32)
    upstream_values = upstream_cols.astype(jnp.float32)
    output_cols = (gate_values * channel_gain * hidden_values).astype(jnp.bfloat16)
    hidden_cols = (upstream_values * gate_values * channel_gain).astype(jnp.bfloat16)
    grad_gate_cols = (upstream_values * channel_gain * hidden_values).astype(jnp.bfloat16)
    partial_gain = jnp.sum(upstream_values * gate_values * hidden_values, axis=(0, 1))
    grad_pairs = jnp.einsum(
        "ajc,bjc->jab", hidden_cols, columns, preferred_element_type=jnp.float32
    )
    grad_sec = jnp.where(mask_second[None], grad_pairs, jnp.zeros((), jnp.float32)).astype(
        jnp.bfloat16
    )
    back_cols = jnp.einsum(
        "jab,ajc->bjc", second_masked, hidden_cols, preferred_element_type=jnp.float32
    ).astype(jnp.bfloat16)
    back_rows, output_rows, grad_gate_rows = (
        lax.all_to_all(back_cols, "seq", split_axis=0, concat_axis=1, tiled=True),
        lax.all_to_all(output_cols, "seq", split_axis=0, concat_axis=1, tiled=True),
        lax.all_to_all(grad_gate_cols, "seq", split_axis=0, concat_axis=1, tiled=True),
    )
    gain_grad = lax.psum(partial_gain, "seq") * norm_factor
    grad_pairs_first = jnp.einsum(
        "kac,kbc->kab", back_rows, rows3, preferred_element_type=jnp.float32
    )
    grad_first = jnp.where(mask_first[None], grad_pairs_first, jnp.zeros((), jnp.float32)).astype(
        jnp.bfloat16
    )
    grad_in = jnp.einsum(
        "kab,kac->kbc", first_masked, back_rows, preferred_element_type=jnp.float32
    ).astype(jnp.bfloat16)
    token_rows = inputs.shape[0]
    return (
        output_rows.reshape(token_rows, channels),
        grad_in.reshape(token_rows, channels),
        grad_gate_rows.reshape(token_rows, channels),
        grad_first,
        grad_sec,
        gain_grad,
    )


def solution(mesh):
    placed = (
        P(("groups", "seq"), None),
        P(("groups", "seq"), None),
        P(("groups", "seq"), None),
        P("seq", None, None),
        P("seq", None, None),
        P(),
    )
    return jax.shard_map(
        on_device,
        mesh=mesh,
        in_specs=placed,
        out_specs=(
            P(("groups", "seq"), None),
            P(("groups", "seq"), None),
            P(("groups", "seq"), None),
            P(("groups", "seq"), None, None),
            P(("groups", "seq"), None, None),
            P("groups"),
        ),
        check_vma=False,
    )
```

profile of v0, /device:TPU:0, one launch (start us, length us, event | category | flops | bytes accessed | tf_op | source)
XLA Modules:
  0.0 196.3 jit_solution(10928412952804270693)
XLA Ops:
  0.6 1.1 copy-done
  1.8 1.6 fusion.5
  3.4 1.2 copy.83
  5.1 5.4 %reduce.2 = bf16[512,768]{1,0:T(8,128)(2,1)S(1)} reduce(bf16[512,1,768]{2,1,0:T(2,128)(2,1)S(1)} %bitcast.48, bf16[]{:T(256)} %broadcast.2), dimensions={1}, to_apply=%bitcast.46.reduce_sub_computation | reduce | bytes 1572866
  10.6 1.1 reshape.99
  11.6 7.6 %all-to-all-start.1 = ((bf16[16,2,12288]{2,1,0:T(2,128)(2,1)}), bf16[16,2,12288]{2,1,0:T(2,128)(2,1)}, u32[]{:S(2)}, u32[]{:S(2)}) async-start(bf16[16,2,12288]{2,1,0:T(2,128)(2,1)} %reshape.99), calls=%async_computation.1 | async-start | bytes 1572864 | tf_op jit(solution)/shard_map/all_to_all | solution.py:34
  19.2 1.2 copy.84
  20.4 5.4 %reduce = bf16[512,768]{1,0:T(8,128)(2,1)S(1)} reduce(bf16[512,1,768]{2,1,0:T(2,128)(2,1)S(1)} %bitcast.53, bf16[]{:T(256)} %broadcast.2), dimensions={1}, to_apply=%bitcast.47.reduce_sub_computation | reduce | bytes 1572866
  25.9 1.1 reshape.101
  26.9 11.0 %all-to-all-done.1 = bf16[16,2,12288]{2,1,0:T(2,128)(2,1)} async-done(((bf16[16,2,12288]{2,1,0:T(2,128)(2,1)}), bf16[16,2,12288]{2,1,0:T(2,128)(2,1)}, u32[]{:S(2)}, u32[]{:S(2)}) %all-to-all-start.1) | async-done | bytes 786464 | tf_op jit(solution)/shard_map/all_to_all | solution.py:34
  38.0 5.5 %all-to-all-start = ((bf16[16,2,12288]{2,1,0:T(2,128)(2,1)}), bf16[16,2,12288]{2,1,0:T(2,128)(2,1)}, u32[]{:S(2)}, u32[]{:S(2)}) async-start(bf16[16,2,12288]{2,1,0:T(2,128)(2,1)} %reshape.101), calls=%async_computation | async-start | bytes 1572864 | tf_op jit(solution)/shard_map/all_to_all | solution.py:28
  43.5 1.2 copy.82
  44.7 5.4 %reduce.1 = bf16[512,768]{1,0:T(8,128)(2,1)S(1)} reduce(bf16[512,1,768]{2,1,0:T(2,128)(2,1)S(1)} %bitcast.49, bf16[]{:T(256)} %broadcast.2), dimensions={1}, to_apply=%bitcast.45.reduce_sub_computation | reduce | bytes 1572866
  51.2 11.0 %all-to-all-done = bf16[16,2,12288]{2,1,0:T(2,128)(2,1)} async-done(((bf16[16,2,12288]{2,1,0:T(2,128)(2,1)}), bf16[16,2,12288]{2,1,0:T(2,128)(2,1)}, u32[]{:S(2)}, u32[]{:S(2)}) %all-to-all-start) | async-done | bytes 786464 | tf_op jit(solution)/shard_map/all_to_all | solution.py:28
  62.3 5.5 %all-to-all-start.3 = ((bf16[16,2,12288]{2,1,0:T(2,128)(2,1)}), bf16[16,2,12288]{2,1,0:T(2,128)(2,1)S(1)}, u32[]{:S(2)}, u32[]{:S(2)}) async-start(bf16[16,2,12288]{2,1,0:T(2,128)(2,1)} %reshape.103), calls=%async_computation.3 | async-start | bytes 1572864 | tf_op jit(solution)/shard_map/all_to_all | solution.py:29
  67.9 4.4 %reshape.100 = bf16[512,1,768]{2,1,0:T(2,128)(2,1)S(1)} reshape(bf16[16,2,12288]{2,1,0:T(2,128)(2,1)} %all-to-all-done.1) | data formatting | bytes 1572864
  73.3 4.4 %reshape.102 = bf16[512,1,768]{2,1,0:T(2,128)(2,1)S(1)} reshape(bf16[16,2,12288]{2,1,0:T(2,128)(2,1)} %all-to-all-done) | data formatting | bytes 1572864
  77.8 1.3 convert.3
  79.1 7.3 %all-to-all-done.3 = bf16[16,2,12288]{2,1,0:T(2,128)(2,1)S(1)} async-done(((bf16[16,2,12288]{2,1,0:T(2,128)(2,1)}), bf16[16,2,12288]{2,1,0:T(2,128)(2,1)S(1)}, u32[]{:S(2)}, u32[]{:S(2)}) %all-to-all-start.3) | async-done | bytes 786464 | tf_op jit(solution)/shard_map/all_to_all | solution.py:29
  88.9 2.4 %fusion.2 = (f32[768]{0:T(1024)S(1)}, bf16[16,32,768]{2,0,1:T(8,128)(2,1)S(1)}, bf16[16,32,768]{2,0,1:T(8,128)(2,1)S(1)}, bf16[16,32,768]{2,0,1:T(8,128)(2,1)S(1)}) fusion(f32[16,32,768]{2,1,0:T(8,128)S(1)} %copy-done.1, f32[16,32,768]{2,1,0:T(8,128)S(1)} %convert.4, f32[768]{0:T(1024)S(1)} %copy-done.7, bf16[16,32,768]{2,1,0:T(8,128)(2,1)S(1)} %bitcast.58, ...), kind=kOutput, calls=%fused_computation.5 | convolution fusion | flops 17702144 | bytes 6314240 | tf_op jit(solution)/shard_map/jab,bjc->ajc/dot_general | solution.py:35
  92.7 1.1 copy.54
  93.8 5.5 %all-to-all-start.4 = ((bf16[16,32,768]{2,1,0:T(8,128)(2,1)}), bf16[16,32,768]{2,1,0:T(8,128)(2,1)}, u32[]{:S(2)}, u32[]{:S(2)}) async-start(bf16[16,32,768]{2,1,0:T(8,128)(2,1)} %copy.54), calls=%async_computation.4 | async-start | bytes 1572864 | tf_op jit(solution)/shard_map/all_to_all | solution.py:55
  99.3 1.1 copy.56
  100.5 17.7 %all-to-all-done.4 = bf16[16,32,768]{2,1,0:T(8,128)(2,1)} async-done(((bf16[16,32,768]{2,1,0:T(8,128)(2,1)}), bf16[16,32,768]{2,1,0:T(8,128)(2,1)}, u32[]{:S(2)}, u32[]{:S(2)}) %all-to-all-start.4) | async-done | bytes 786464 | tf_op jit(solution)/shard_map/all_to_all | solution.py:55
  118.1 5.5 %all-to-all-start.5 = ((bf16[16,32,768]{2,1,0:T(8,128)(2,1)}), bf16[16,32,768]{2,1,0:T(8,128)(2,1)S(1)}, u32[]{:S(2)}, u32[]{:S(2)}) async-start(bf16[16,32,768]{2,1,0:T(8,128)(2,1)} %copy.56), calls=%async_computation.5 | async-start | bytes 1572864 | tf_op jit(solution)/shard_map/all_to_all | solution.py:57
  123.6 1.1 copy.48
  124.7 17.6 %all-to-all-done.5 = bf16[16,32,768]{2,1,0:T(8,128)(2,1)S(1)} async-done(((bf16[16,32,768]{2,1,0:T(8,128)(2,1)}), bf16[16,32,768]{2,1,0:T(8,128)(2,1)S(1)}, u32[]{:S(2)}, u32[]{:S(2)}) %all-to-all-start.5) | async-done | bytes 786464 | tf_op jit(solution)/shard_map/all_to_all | solution.py:57
  142.3 5.5 %all-to-all-start.2 = ((bf16[16,32,768]{2,1,0:T(8,128)(2,1)}), bf16[16,32,768]{2,1,0:T(8,128)(2,1)S(1)}, u32[]{:S(2)}, u32[]{:S(2)}) async-start(bf16[16,32,768]{2,1,0:T(8,128)(2,1)} %copy.48), calls=%async_computation.2 | async-start | bytes 1572864 | tf_op jit(solution)/shard_map/all_to_all | solution.py:56
  147.8 1.7 fusion.7
  150.3 38.5 %psum.7 = f32[768]{0:T(1024)S(1)} all-reduce(f32[768]{0:T(1024)S(1)} %get-tuple-element.30), channel_id=1, replica_groups=mesh['groups'=2,'seq'=16] {'seq'}, use_global_device_ids=true, to_apply=%region_1.2 | all-reduce | flops 768 | bytes 6144 | tf_op jit(solution)/shard_map/psum | solution.py:59
  189.4 2.5 %fusion.6 = bf16[1,512,512]{2,1,0:T(8,128)(2,1)} fusion(bf16[512,768]{1,0:T(8,128)(2,1)} %bitcast.10, bf16[512,768]{1,0:T(8,128)(2,1)S(1)} %copy-done), kind=kOutput, calls=%fused_computation.16 | convolution fusion | flops 403439616 | bytes 2097152 | tf_op jit(solution)/shard_map/kac,kbc->kab/dot_general | solution.py:60
  191.9 2.6 %convolution_convert_fusion = bf16[512,768]{1,0:T(8,128)(2,1)} fusion(bf16[512,768]{1,0:T(8,128)(2,1)} %bitcast.10, bf16[1,512,512]{2,1,0:T(8,128)(2,1)S(1)} %copy-done.8), kind=kOutput, calls=%fused_computation.8 | convolution fusion | flops 403570688 | bytes 2097152 | tf_op jit(solution)/shard_map/kab,kac->kbc/dot_general | solution.py:66
  (32 shorter events, 9.8 us)
Async XLA Ops:
  0.6 1.1 copy-start
  11.6 7.6 %copy-start.4 = (bf16[512,768]{1,0:T(8,128)(2,1)S(1)}, bf16[512,768]{1,0:T(8,128)(2,1)}, u32[]{:S(2)}) copy-start(bf16[512,768]{1,0:T(8,128)(2,1)} %param.7) | copy-start | bytes 2359300
  11.6 26.3 %all-to-all-start.1 = ((bf16[16,2,12288]{2,1,0:T(2,128)(2,1)}), bf16[16,2,12288]{2,1,0:T(2,128)(2,1)}, u32[]{:S(2)}, u32[]{:S(2)}) async-start(bf16[16,2,12288]{2,1,0:T(2,128)(2,1)} %reshape.99), calls=%async_computation.1 | async-start | bytes 1572864 | tf_op jit(solution)/shard_map/all_to_all | solution.py:34
  26.9 16.6 %copy-start.5 = (bf16[512,768]{1,0:T(8,128)(2,1)S(1)}, bf16[512,768]{1,0:T(8,128)(2,1)}, u32[]{:S(2)}) copy-start(bf16[512,768]{1,0:T(8,128)(2,1)} %param.8) | copy-start | bytes 2359300
  38.0 24.3 %all-to-all-start = ((bf16[16,2,12288]{2,1,0:T(2,128)(2,1)}), bf16[16,2,12288]{2,1,0:T(2,128)(2,1)}, u32[]{:S(2)}, u32[]{:S(2)}) async-start(bf16[16,2,12288]{2,1,0:T(2,128)(2,1)} %reshape.101), calls=%async_computation | async-start | bytes 1572864 | tf_op jit(solution)/shard_map/all_to_all | solution.py:28
  50.2 17.6 %copy-start.6 = (bf16[32,16,16]{0,2,1:T(8,128)(2,1)S(1)}, bf16[32,16,16]{0,2,1:T(8,128)(2,1)}, u32[]{:S(2)}) copy-start(bf16[32,16,16]{0,2,1:T(8,128)(2,1)} %param.10) | copy-start | bytes 49156
  62.3 24.2 %all-to-all-start.3 = ((bf16[16,2,12288]{2,1,0:T(2,128)(2,1)}), bf16[16,2,12288]{2,1,0:T(2,128)(2,1)S(1)}, u32[]{:S(2)}, u32[]{:S(2)}) async-start(bf16[16,2,12288]{2,1,0:T(2,128)(2,1)} %reshape.103), calls=%async_computation.3 | async-start | bytes 1572864 | tf_op jit(solution)/shard_map/all_to_all | solution.py:29
  87.2 0.7 copy-start.7
  87.3 1.4 copy-start.1
  87.3 1.6 copy-start.2
  91.4 0.9 copy-start.3
  93.8 24.3 %all-to-all-start.4 = ((bf16[16,32,768]{2,1,0:T(8,128)(2,1)}), bf16[16,32,768]{2,1,0:T(8,128)(2,1)}, u32[]{:S(2)}, u32[]{:S(2)}) async-start(bf16[16,32,768]{2,1,0:T(8,128)(2,1)} %copy.54), calls=%async_computation.4 | async-start | bytes 1572864 | tf_op jit(solution)/shard_map/all_to_all | solution.py:55
  118.1 24.2 %all-to-all-start.5 = ((bf16[16,32,768]{2,1,0:T(8,128)(2,1)}), bf16[16,32,768]{2,1,0:T(8,128)(2,1)S(1)}, u32[]{:S(2)}, u32[]{:S(2)}) async-start(bf16[16,32,768]{2,1,0:T(8,128)(2,1)} %copy.56), calls=%async_computation.5 | async-start | bytes 1572864 | tf_op jit(solution)/shard_map/all_to_all | solution.py:57
  142.3 52.2 %all-to-all-start.2 = ((bf16[16,32,768]{2,1,0:T(8,128)(2,1)}), bf16[16,32,768]{2,1,0:T(8,128)(2,1)S(1)}, u32[]{:S(2)}, u32[]{:S(2)}) async-start(bf16[16,32,768]{2,1,0:T(8,128)(2,1)} %copy.48), calls=%async_computation.2 | async-start | bytes 1572864 | tf_op jit(solution)/shard_map/all_to_all | solution.py:56
  149.5 42.4 %copy-start.8 = (bf16[1,512,512]{2,1,0:T(8,128)(2,1)S(1)}, bf16[1,512,512]{2,1,0:T(8,128)(2,1)}, u32[]{:S(2)}) copy-start(bf16[1,512,512]{2,1,0:T(8,128)(2,1)} %param.9) | copy-start | bytes 1572868
where the time goes:
time: 197 us; the launch traced here: 196 us
  waiting for transfers between devices  64.6 us (33%)
  blocking collectives  38.5 us (20%)
  starting transfers between devices  35.1 us (18%)
  local copies, waits for them, and re-layouts  27.5 us (14%)
  other arithmetic  18.3 us (9%)
  matrix products  11.3 us (6%)
    psum x1, blocking collectives, on_device(): gain_grad = lax.psum(partial_gain, 'seq') * norm_factor  38.5 us
    unnamed x30, local copies, waits for them, and re-layouts  20.3 us
    all_to_all x1, waiting for transfers between devices, on_device(): lax.all_to_all(back_cols, 'seq', split_axis=0, concat_axis=1, tiled=True)  17.7 us
    all_to_all x1, waiting for transfers between devices, on_device(): lax.all_to_all(grad_gate_cols, 'seq', split_axis=0, concat_axis=1, tiled=...  17.6 us
    unnamed x3, other arithmetic  16.3 us
    all_to_all x1, waiting for transfers between devices, on_device(): lax.all_to_all(first_mixed, 'seq', split_axis=1, concat_axis=0, tiled=True)  11 us
    all_to_all x1, waiting for transfers between devices, on_device(): lax.all_to_all(gates3, 'seq', split_axis=1, concat_axis=0, tiled=True)  11 us
    all_to_all x1, starting transfers between devices, on_device(): lax.all_to_all(first_mixed, 'seq', split_axis=1, concat_axis=0, tiled=True)  7.57 us
  transfers between devices with their start and end apart: 6, of which 5 were waited for; matrix products, arithmetic and copies ran while one was open for 19% of the time, Pallas kernels for 0%

commit v1 on v0

--- a/solution.py
+++ b/solution.py
@@ -3,6 +3,29 @@
 import jax.numpy as jnp
 from jax import lax
 from jax.sharding import PartitionSpec as P
+
+
+def in_blocks(x, dim, count):
+    lengths = x.shape
+    blocks = x.reshape(*lengths[:dim], count, lengths[dim] // count, *lengths[dim + 1 :])
+    return jnp.moveaxis(blocks, dim, 0)
+
+
+def laid_out(blocks, dim):
+    shape = list(blocks.shape[1:])
+    shape[dim] *= blocks.shape[0]
+    return jnp.moveaxis(blocks, 0, dim).reshape(shape)
+
+
+def pairwise_exchange(value, axis, split_dim, concat_dim):
+    peers, index = (lax.axis_size(axis), lax.axis_index(axis))
+    pieces = in_blocks(value, split_dim, peers)
+    outs = [pieces[index]]
+    for step in range(1, peers):
+        sent = pieces[index ^ step]
+        outs.append(lax.ppermute(sent, axis, [(i, i ^ step) for i in range(peers)]))
+    pieces = jnp.stack(outs)[index ^ jnp.arange(peers)]
+    return laid_out(pieces, concat_dim)
 
 
 def lower_mask(extent):
@@ -26,7 +49,7 @@
     norm_factor = 1.0 / math.sqrt(inputs.shape[0] * lax.axis_size("seq"))
     gates_cols, upstream_cols = (
         lax.all_to_all(gates3, "seq", split_axis=1, concat_axis=0, tiled=True),
-        lax.all_to_all(upstream3, "seq", split_axis=1, concat_axis=0, tiled=True),
+        pairwise_exchange(upstream3, "seq", 1, 0),
     )
     first_mixed = jnp.einsum(
         "kab,kbc->kac", first_masked, rows3, preferred_element_type=jnp.float32

time: 197 us -> 220 us (1.12)
  waiting for transfers between devices: 64.6 us -> 82.9 us
  starting transfers between devices: 35.1 us -> 47.1 us
  other arithmetic: 18.3 us -> 11.6 us
    ppermute x0 -> x15, waiting for transfers between devices: none -> 47.8 us  [pairwise_exchange(): outs.append(lax.ppermute(sent, axis, [(i, i ^ step) for i in range(peers)]))]
    ppermute x0 -> x15, starting transfers between devices: none -> 20.7 us  [pairwise_exchange(): outs.append(lax.ppermute(sent, axis, [(i, i ^ step) for i in range(peers)]))]
    all_to_all x1, waiting for transfers between devices: 17.6 us -> 0.01 us  [on_device(): lax.all_to_all(grad_gate_cols, 'seq', split_axis=0, concat_axis=1, tiled=...]
    all_to_all x1, waiting for transfers between devices: 0.01 us -> 17.6 us  [on_device(): lax.all_to_all(output_cols, 'seq', split_axis=0, concat_axis=1, tiled=True)]
    all_to_all x1, waiting for transfers between devices: 11 us -> 0.01 us  [on_device(): lax.all_to_all(first_mixed, 'seq', split_axis=1, concat_axis=0, tiled=True)]
    all_to_all x1, waiting for transfers between devices: 11 us -> 0.01 us  [on_device(): lax.all_to_all(gates3, 'seq', split_axis=1, concat_axis=0, tiled=True)]
    all_to_all x1 -> x0, waiting for transfers between devices: 7.34 us -> none  [on_device(): lax.all_to_all(upstream3, 'seq', split_axis=1, concat_axis=0, tiled=True)]
    all_to_all x1 -> x0, starting transfers between devices: 5.48 us -> none  [on_device(): lax.all_to_all(upstream3, 'seq', split_axis=1, concat_axis=0, tiled=True)]
  transfers between devices with their start and end apart: 6 -> 20, of which waited for: 5 -> 12; matrix products, arithmetic and copies ran while one was open for 19% -> 13% of each run, Pallas kernels for 0% -> 0%
where the time goes in v1:
time: 220 us; the launch traced here: 219 us
  waiting for transfers between devices  82.9 us (38%)
  starting transfers between devices  47.1 us (21%)
  blocking collectives  38.2 us (17%)
  local copies, waits for them, and re-layouts  26.2 us (12%)
  other arithmetic  11.6 us (5%)
  matrix products  11.5 us (5%)
    ppermute x15, waiting for transfers between devices, pairwise_exchange(): outs.append(lax.ppermute(sent, axis, [(i, i ^ step) for i in range(peers)]))  47.8 us
    psum x1, blocking collectives, on_device(): gain_grad = lax.psum(partial_gain, 'seq') * norm_factor  38.2 us
    ppermute x15, starting transfers between devices, pairwise_exchange(): outs.append(lax.ppermute(sent, axis, [(i, i ^ step) for i in range(peers)]))  20.7 us
    all_to_all x1, waiting for transfers between devices, on_device(): lax.all_to_all(output_cols, 'seq', split_axis=0, concat_axis=1, tiled=True)  17.6 us
    all_to_all x1, waiting for transfers between devices, on_device(): lax.all_to_all(back_cols, 'seq', split_axis=0, concat_axis=1, tiled=True)  17.5 us
    unnamed x62, local copies, waits for them, and re-layouts  17.1 us
    unnamed x2, other arithmetic  10.9 us
    all_to_all x1, starting transfers between devices, on_device(): lax.all_to_all(first_mixed, 'seq', split_axis=1, concat_axis=0, tiled=True)  7.57 us
  transfers between devices with their start and end apart: 20, of which 12 were waited for; matrix products, arithmetic and copies ran while one was open for 13% of the time, Pallas kernels for 0%

profile of v1, /device:TPU:0, one launch (start us, length us, event | category | flops | bytes accessed | tf_op | source)
XLA Modules:
  0.0 218.6 jit_solution(8174384369541128060)
XLA Ops:
  1.8 1.6 fusion.6
  5.1 5.4 %reduce.1 = bf16[512,768]{1,0:T(8,128)(2,1)S(1)} reduce(bf16[512,1,768]{2,1,0:T(2,128)(2,1)S(1)} %bitcast.103, bf16[]{:T(256)} %broadcast.37), dimensions={1}, to_apply=%bitcast.101.reduce_sub_computation | reduce | bytes 1572866
  11.6 7.6 %all-to-all-start.1 = ((bf16[16,2,12288]{2,1,0:T(2,128)(2,1)}), bf16[16,2,12288]{2,1,0:T(2,128)(2,1)}, u32[]{:S(2)}, u32[]{:S(2)}) async-start(bf16[16,2,12288]{2,1,0:T(2,128)(2,1)} %reshape.121), calls=%async_computation.1 | async-start | bytes 1572864 | tf_op jit(solution)/shard_map/all_to_all | solution.py:57
  20.1 4.2 %collective-permute-start.14 = (bf16[1,32,768]{2,1,0:T(8,128)(2,1)S(1)}, bf16[1,32,768]{2,1,0:T(8,128)(2,1)}, u32[]{:S(2)}, u32[]{:S(2)}) collective-permute-start(bf16[1,32,768]{2,1,0:T(8,128)(2,1)S(1)} %get-tuple-element.34), channel_id=1, source_target_pairs={{0,15},{1,14},{2,13},{3,12},{4,11},{5,10},{6,9},{7,8},{8,7},{9,6},... | collective-permute-start | bytes 147464 | tf_op jit(solution)/shard_map/ppermute | solution.py:26
  24.7 3.2 %collective-permute-start.12 = (bf16[1,32,768]{2,1,0:T(8,128)(2,1)S(1)}, bf16[1,32,768]{2,1,0:T(8,128)(2,1)}, u32[]{:S(2)}, u32[]{:S(2)}) collective-permute-start(bf16[1,32,768]{2,1,0:T(8,128)(2,1)S(1)} %get-tuple-element.36), channel_id=1, source_target_pairs={{0,13},{1,12},{2,15},{3,14},{4,9},{5,8},{6,11},{7,10},{8,5},{9,4},... | collective-permute-start | bytes 147464 | tf_op jit(solution)/shard_map/ppermute | solution.py:26
  29.9 5.4 %reduce = bf16[512,768]{1,0:T(8,128)(2,1)S(1)} reduce(bf16[512,1,768]{2,1,0:T(2,128)(2,1)S(1)} %bitcast.104, bf16[]{:T(256)} %broadcast.37), dimensions={1}, to_apply=%bitcast.102.reduce_sub_computation | reduce | bytes 1572866
  36.5 1.7 collective-permute-start.1
  38.9 2.1 collective-permute-done.1
  41.4 3.5 %collective-permute-done.2 = bf16[1,32,768]{2,1,0:T(8,128)(2,1)S(1)} collective-permute-done((bf16[1,32,768]{2,1,0:T(8,128)(2,1)S(1)}, bf16[1,32,768]{2,1,0:T(8,128)(2,1)S(1)}, u32[]{:S(2)}, u32[]{:S(2)}) %collective-permute-start.2) | collective-permute-done | bytes 49184 | tf_op jit(solution)/shard_map/ppermute | solution.py:26
  45.0 4.1 %collective-permute-done.3 = bf16[1,32,768]{2,1,0:T(8,128)(2,1)S(1)} collective-permute-done((bf16[1,32,768]{2,1,0:T(8,128)(2,1)S(1)}, bf16[1,32,768]{2,1,0:T(8,128)(2,1)S(1)}, u32[]{:S(2)}, u32[]{:S(2)}) %collective-permute-start.3) | collective-permute-done | bytes 49184 | tf_op jit(solution)/shard_map/ppermute | solution.py:26
  49.1 3.5 %collective-permute-done.4 = bf16[1,32,768]{2,1,0:T(8,128)(2,1)S(1)} collective-permute-done((bf16[1,32,768]{2,1,0:T(8,128)(2,1)S(1)}, bf16[1,32,768]{2,1,0:T(8,128)(2,1)S(1)}, u32[]{:S(2)}, u32[]{:S(2)}) %collective-permute-start.4) | collective-permute-done | bytes 49184 | tf_op jit(solution)/shard_map/ppermute | solution.py:26
  53.1 4.4 %collective-permute-done.5 = bf16[1,32,768]{2,1,0:T(8,128)(2,1)S(1)} collective-permute-done((bf16[1,32,768]{2,1,0:T(8,128)(2,1)S(1)}, bf16[1,32,768]{2,1,0:T(8,128)(2,1)S(1)}, u32[]{:S(2)}, u32[]{:S(2)}) %collective-permute-start.5) | collective-permute-done | bytes 49184 | tf_op jit(solution)/shard_map/ppermute | solution.py:26
  57.6 4.4 %collective-permute-done.6 = bf16[1,32,768]{2,1,0:T(8,128)(2,1)S(1)} collective-permute-done((bf16[1,32,768]{2,1,0:T(8,128)(2,1)S(1)}, bf16[1,32,768]{2,1,0:T(8,128)(2,1)S(1)}, u32[]{:S(2)}, u32[]{:S(2)}) %collective-permute-start.6) | collective-permute-done | bytes 49184 | tf_op jit(solution)/shard_map/ppermute | solution.py:26
  62.0 2.7 %collective-permute-start.7 = (bf16[1,32,768]{2,1,0:T(8,128)(2,1)S(1)}, bf16[1,32,768]{2,1,0:T(8,128)(2,1)S(1)}, u32[]{:S(2)}, u32[]{:S(2)}) collective-permute-start(bf16[1,32,768]{2,1,0:T(8,128)(2,1)S(1)} %copy-done.10), channel_id=1, source_target_pairs={{0,8},{1,9},{2,10},{3,11},{4,12},{5,13},{6,14},{7,15},{8,0},{9,1},... | collective-permute-start | bytes 147464 | tf_op jit(solution)/shard_map/ppermute | solution.py:26
  64.7 2.2 %collective-permute-done.7 = bf16[1,32,768]{2,1,0:T(8,128)(2,1)S(1)} collective-permute-done((bf16[1,32,768]{2,1,0:T(8,128)(2,1)S(1)}, bf16[1,32,768]{2,1,0:T(8,128)(2,1)S(1)}, u32[]{:S(2)}, u32[]{:S(2)}) %collective-permute-start.7) | collective-permute-done | bytes 49184 | tf_op jit(solution)/shard_map/ppermute | solution.py:26
  68.2 3.3 %collective-permute-done.8 = bf16[1,32,768]{2,1,0:T(8,128)(2,1)S(1)} collective-permute-done((bf16[1,32,768]{2,1,0:T(8,128)(2,1)S(1)}, bf16[1,32,768]{2,1,0:T(8,128)(2,1)S(1)}, u32[]{:S(2)}, u32[]{:S(2)}) %collective-permute-start.8) | collective-permute-done | bytes 49184 | tf_op jit(solution)/shard_map/ppermute | solution.py:26
  71.6 2.6 %collective-permute-start.9 = (bf16[1,32,768]{2,1,0:T(8,128)(2,1)S(1)}, bf16[1,32,768]{2,1,0:T(8,128)(2,1)S(1)}, u32[]{:S(2)}, u32[]{:S(2)}) collective-permute-start(bf16[1,32,768]{2,1,0:T(8,128)(2,1)S(1)} %copy-done.8), channel_id=1, source_target_pairs={{0,10},{1,11},{2,8},{3,9},{4,14},{5,15},{6,12},{7,13},{8,2},{9,3},... | collective-permute-start | bytes 147464 | tf_op jit(solution)/shard_map/ppermute | solution.py:26
  74.2 4.3 %all-to-all-start = ((bf16[16,2,12288]{2,1,0:T(2,128)(2,1)}), bf16[16,2,12288]{2,1,0:T(2,128)(2,1)S(1)}, u32[]{:S(2)}, u32[]{:S(2)}) async-start(bf16[16,2,12288]{2,1,0:T(2,128)(2,1)} %reshape.123), calls=%async_computation | async-start | bytes 1572864 | tf_op jit(solution)/shard_map/all_to_all | solution.py:51
  78.8 3.3 %collective-permute-start.10 = (bf16[1,32,768]{2,1,0:T(8,128)(2,1)S(1)}, bf16[1,32,768]{2,1,0:T(8,128)(2,1)S(1)}, u32[]{:S(2)}, u32[]{:S(2)}) collective-permute-start(bf16[1,32,768]{2,1,0:T(8,128)(2,1)S(1)} %get-tuple-element.38), channel_id=1, source_target_pairs={{0,11},{1,10},{2,9},{3,8},{4,15},{5,14},{6,13},{7,12},{8,3},{9,2},... | collective-permute-start | bytes 147464 | tf_op jit(solution)/shard_map/ppermute | solution.py:26
  82.0 19.9 %collective-permute-done.10 = bf16[1,32,768]{2,1,0:T(8,128)(2,1)S(1)} collective-permute-done((bf16[1,32,768]{2,1,0:T(8,128)(2,1)S(1)}, bf16[1,32,768]{2,1,0:T(8,128)(2,1)S(1)}, u32[]{:S(2)}, u32[]{:S(2)}) %collective-permute-start.10) | collective-permute-done | bytes 49184 | tf_op jit(solution)/shard_map/ppermute | solution.py:26
  105.1 1.5 gather_fusion
  106.6 4.4 %reshape.122 = bf16[512,1,768]{2,1,0:T(2,128)(2,1)S(1)} reshape(bf16[16,2,12288]{2,1,0:T(2,128)(2,1)} %all-to-all-done.1) | data formatting | bytes 1572864
  114.2 3.5 %fusion.3 = (f32[768]{0:T(1024)S(1)}, bf16[16,32,768]{2,0,1:T(8,128)(2,1)}, bf16[16,32,768]{2,0,1:T(8,128)(2,1)}, bf16[16,32,768]{2,0,1:T(8,128)(2,1)S(1)}) fusion(f32[16,32,768]{2,1,0:T(8,128)S(1)} %convert.3, bf16[16,32,768]{2,1,0:T(8,128)(2,1)S(1)} %copy-done.3, f32[768]{0:T(1024)S(1)} %copy-done.18, bf16[16,32,768]{2,1,0:T(8,128)(2,1)S(1)} %bitcast.116, ...), kind=kOutput, calls=%fused_computation.8 | convolution fusion | flops 18095360 | bytes 5527808 | tf_op jit(solution)/shard_map/jab,bjc->ajc/dot_general | solution.py:58
  117.7 1.5 fusion.5
  120.4 3.6 %all-to-all-start.3 = ((bf16[16,32,768]{2,1,0:T(8,128)(2,1)}), bf16[16,32,768]{2,1,0:T(8,128)(2,1)S(1)}, u32[]{:S(2)}, u32[]{:S(2)}) async-start(bf16[16,32,768]{2,1,0:T(8,128)(2,1)} %copy.49), calls=%async_computation.3 | async-start | bytes 1572864 | tf_op jit(solution)/shard_map/all_to_all | solution.py:78
  125.1 17.5 %all-to-all-done.3 = bf16[16,32,768]{2,1,0:T(8,128)(2,1)S(1)} async-done(((bf16[16,32,768]{2,1,0:T(8,128)(2,1)}), bf16[16,32,768]{2,1,0:T(8,128)(2,1)S(1)}, u32[]{:S(2)}, u32[]{:S(2)}) %all-to-all-start.3) | async-done | bytes 786464 | tf_op jit(solution)/shard_map/all_to_all | solution.py:78
  142.7 5.4 %all-to-all-start.2 = ((bf16[16,32,768]{2,1,0:T(8,128)(2,1)}), bf16[16,32,768]{2,1,0:T(8,128)(2,1)S(1)}, u32[]{:S(2)}, u32[]{:S(2)}) async-start(bf16[16,32,768]{2,1,0:T(8,128)(2,1)} %copy.45), calls=%async_computation.2 | async-start | bytes 1572864 | tf_op jit(solution)/shard_map/all_to_all | solution.py:79
  149.3 17.6 %all-to-all-done.2 = bf16[16,32,768]{2,1,0:T(8,128)(2,1)S(1)} async-done(((bf16[16,32,768]{2,1,0:T(8,128)(2,1)}), bf16[16,32,768]{2,1,0:T(8,128)(2,1)S(1)}, u32[]{:S(2)}, u32[]{:S(2)}) %all-to-all-start.2) | async-done | bytes 786464 | tf_op jit(solution)/shard_map/all_to_all | solution.py:79
  166.8 5.5 %all-to-all-start.4 = ((bf16[16,32,768]{2,1,0:T(8,128)(2,1)}), bf16[16,32,768]{2,1,0:T(8,128)(2,1)S(1)}, u32[]{:S(2)}, u32[]{:S(2)}) async-start(bf16[16,32,768]{2,1,0:T(8,128)(2,1)} %copy.50), calls=%async_computation.4 | async-start | bytes 1572864 | tf_op jit(solution)/shard_map/all_to_all | solution.py:80
  172.3 2.0 fusion.8
  175.1 38.2 %psum.7 = f32[768]{0:T(1024)S(1)} all-reduce(f32[768]{0:T(1024)S(1)} %get-tuple-element.30), channel_id=1, replica_groups=mesh['groups'=2,'seq'=16] {'seq'}, use_global_device_ids=true, to_apply=%region_1.2 | all-reduce | flops 768 | bytes 6144 | tf_op jit(solution)/shard_map/psum | solution.py:82
  215.3 1.5 convolution_convert_fusion
  (93 shorter events, 25.9 us)
Async XLA Ops:
  10.6 8.7 %copy-start.2 = (bf16[512,768]{1,0:T(8,128)(2,1)S(1)}, bf16[512,768]{1,0:T(8,128)(2,1)}, u32[]{:S(2)}) copy-start(bf16[512,768]{1,0:T(8,128)(2,1)} %param.8) | copy-start | bytes 2359300
  11.6 16.8 %copy-start.7 = (bf16[32,16,16]{0,2,1:T(8,128)(2,1)S(1)}, bf16[32,16,16]{0,2,1:T(8,128)(2,1)}, u32[]{:S(2)}) copy-start(bf16[32,16,16]{0,2,1:T(8,128)(2,1)} %param.10) | copy-start | bytes 49156
  11.6 17.0 %copy-start.5 = (bf16[512,768]{1,0:T(8,128)(2,1)S(1)}, bf16[512,768]{1,0:T(8,128)(2,1)}, u32[]{:S(2)}) copy-start(bf16[512,768]{1,0:T(8,128)(2,1)} %param.7) | copy-start | bytes 2359300
  11.6 62.5 %all-to-all-start.1 = ((bf16[16,2,12288]{2,1,0:T(2,128)(2,1)}), bf16[16,2,12288]{2,1,0:T(2,128)(2,1)}, u32[]{:S(2)}, u32[]{:S(2)}) async-start(bf16[16,2,12288]{2,1,0:T(2,128)(2,1)} %reshape.121), calls=%async_computation.1 | async-start | bytes 1572864 | tf_op jit(solution)/shard_map/all_to_all | solution.py:57
  20.1 84.2 %collective-permute-start.14 = (bf16[1,32,768]{2,1,0:T(8,128)(2,1)S(1)}, bf16[1,32,768]{2,1,0:T(8,128)(2,1)}, u32[]{:S(2)}, u32[]{:S(2)}) collective-permute-start(bf16[1,32,768]{2,1,0:T(8,128)(2,1)S(1)} %get-tuple-element.34), channel_id=1, source_target_pairs={{0,15},{1,14},{2,13},{3,12},{4,11},{5,10},{6,9},{7,8},{8,7},{9,6},... | collective-permute-start | bytes 147464 | tf_op jit(solution)/shard_map/ppermute | solution.py:26
  24.4 79.1 %collective-permute-start.13 = (bf16[1,32,768]{2,1,0:T(8,128)(2,1)S(1)}, bf16[1,32,768]{2,1,0:T(8,128)(2,1)}, u32[]{:S(2)}, u32[]{:S(2)}) collective-permute-start(bf16[1,32,768]{2,1,0:T(8,128)(2,1)S(1)} %get-tuple-element.35), channel_id=1, source_target_pairs={{0,14},{1,15},{2,12},{3,13},{4,10},{5,11},{6,8},{7,9},{8,6},{9,7},... | collective-permute-start | bytes 147464 | tf_op jit(solution)/shard_map/ppermute | solution.py:26
  24.7 78.0 %collective-permute-start.12 = (bf16[1,32,768]{2,1,0:T(8,128)(2,1)S(1)}, bf16[1,32,768]{2,1,0:T(8,128)(2,1)}, u32[]{:S(2)}, u32[]{:S(2)}) collective-permute-start(bf16[1,32,768]{2,1,0:T(8,128)(2,1)S(1)} %get-tuple-element.36), channel_id=1, source_target_pairs={{0,13},{1,12},{2,15},{3,14},{4,9},{5,8},{6,11},{7,10},{8,5},{9,4},... | collective-permute-start | bytes 147464 | tf_op jit(solution)/shard_map/ppermute | solution.py:26
  27.9 74.0 %collective-permute-start.11 = (bf16[1,32,768]{2,1,0:T(8,128)(2,1)S(1)}, bf16[1,32,768]{2,1,0:T(8,128)(2,1)}, u32[]{:S(2)}, u32[]{:S(2)}) collective-permute-start(bf16[1,32,768]{2,1,0:T(8,128)(2,1)S(1)} %get-tuple-element.37), channel_id=1, source_target_pairs={{0,12},{1,13},{2,14},{3,15},{4,8},{5,9},{6,10},{7,11},{8,4},{9,5},... | collective-permute-start | bytes 147464 | tf_op jit(solution)/shard_map/ppermute | solution.py:26
  28.3 8.2 %collective-permute-start = (bf16[1,32,768]{2,1,0:T(8,128)(2,1)}, bf16[1,32,768]{2,1,0:T(8,128)(2,1)}, u32[]{:S(2)}, u32[]{:S(2)}) collective-permute-start(bf16[1,32,768]{2,1,0:T(8,128)(2,1)} %get-tuple-element.48), channel_id=1, source_target_pairs={{0,1},{1,0},{2,3},{3,2},{4,5},{5,4},{6,7},{7,6},{8,9},{9,8},{10,11... | collective-permute-start | bytes 147464 | tf_op jit(solution)/shard_map/ppermute | solution.py:26
  35.3 5.7 %copy-start.15 = (bf16[1,32,768]{2,1,0:T(8,128)(2,1)S(1)}, bf16[1,32,768]{2,1,0:T(8,128)(2,1)}, u32[]{:S(2)}) copy-start(bf16[1,32,768]{2,1,0:T(8,128)(2,1)} %get-tuple-element.46) | copy-start | bytes 147460
  35.3 9.6 %copy-start.14 = (bf16[1,32,768]{2,1,0:T(8,128)(2,1)S(1)}, bf16[1,32,768]{2,1,0:T(8,128)(2,1)}, u32[]{:S(2)}) copy-start(bf16[1,32,768]{2,1,0:T(8,128)(2,1)} %get-tuple-element.45) | copy-start | bytes 147460
  35.3 13.7 %copy-start.13 = (bf16[1,32,768]{2,1,0:T(8,128)(2,1)S(1)}, bf16[1,32,768]{2,1,0:T(8,128)(2,1)}, u32[]{:S(2)}) copy-start(bf16[1,32,768]{2,1,0:T(8,128)(2,1)} %get-tuple-element.44) | copy-start | bytes 147460
  35.3 17.2 %copy-start.12 = (bf16[1,32,768]{2,1,0:T(8,128)(2,1)S(1)}, bf16[1,32,768]{2,1,0:T(8,128)(2,1)}, u32[]{:S(2)}) copy-start(bf16[1,32,768]{2,1,0:T(8,128)(2,1)} %get-tuple-element.43) | copy-start | bytes 147460
  35.4 22.2 %copy-start.11 = (bf16[1,32,768]{2,1,0:T(8,128)(2,1)S(1)}, bf16[1,32,768]{2,1,0:T(8,128)(2,1)}, u32[]{:S(2)}) copy-start(bf16[1,32,768]{2,1,0:T(8,128)(2,1)} %get-tuple-element.42) | copy-start | bytes 147460
  35.4 26.6 %copy-start.10 = (bf16[1,32,768]{2,1,0:T(8,128)(2,1)S(1)}, bf16[1,32,768]{2,1,0:T(8,128)(2,1)}, u32[]{:S(2)}) copy-start(bf16[1,32,768]{2,1,0:T(8,128)(2,1)} %get-tuple-element.41) | copy-start | bytes 147460
  35.4 31.6 %copy-start.9 = (bf16[1,32,768]{2,1,0:T(8,128)(2,1)S(1)}, bf16[1,32,768]{2,1,0:T(8,128)(2,1)}, u32[]{:S(2)}) copy-start(bf16[1,32,768]{2,1,0:T(8,128)(2,1)} %get-tuple-element.40) | copy-start | bytes 147460
  35.4 36.2 %copy-start.8 = (bf16[1,32,768]{2,1,0:T(8,128)(2,1)S(1)}, bf16[1,32,768]{2,1,0:T(8,128)(2,1)}, u32[]{:S(2)}) copy-start(bf16[1,32,768]{2,1,0:T(8,128)(2,1)} %get-tuple-element.39) | copy-start | bytes 147460
  36.5 4.6 %collective-permute-start.1 = (bf16[1,32,768]{2,1,0:T(8,128)(2,1)S(1)}, bf16[1,32,768]{2,1,0:T(8,128)(2,1)S(1)}, u32[]{:S(2)}, u32[]{:S(2)}) collective-permute-start(bf16[1,32,768]{2,1,0:T(8,128)(2,1)S(1)} %copy-done.16), channel_id=1, source_target_pairs={{0,2},{1,3},{2,0},{3,1},{4,6},{5,7},{6,4},{7,5},{8,10},{9,11},{10,... | collective-permute-start | bytes 147464 | tf_op jit(solution)/shard_map/ppermute | solution.py:26
  41.0 3.9 %collective-permute-start.2 = (bf16[1,32,768]{2,1,0:T(8,128)(2,1)S(1)}, bf16[1,32,768]{2,1,0:T(8,128)(2,1)S(1)}, u32[]{:S(2)}, u32[]{:S(2)}) collective-permute-start(bf16[1,32,768]{2,1,0:T(8,128)(2,1)S(1)} %copy-done.15), channel_id=1, source_target_pairs={{0,3},{1,2},{2,1},{3,0},{4,7},{5,6},{6,5},{7,4},{8,11},{9,10},{10,... | collective-permute-start | bytes 147464 | tf_op jit(solution)/shard_map/ppermute | solution.py:26
  44.9 4.1 %collective-permute-start.3 = (bf16[1,32,768]{2,1,0:T(8,128)(2,1)S(1)}, bf16[1,32,768]{2,1,0:T(8,128)(2,1)S(1)}, u32[]{:S(2)}, u32[]{:S(2)}) collective-permute-start(bf16[1,32,768]{2,1,0:T(8,128)(2,1)S(1)} %copy-done.14), channel_id=1, source_target_pairs={{0,4},{1,5},{2,6},{3,7},{4,0},{5,1},{6,2},{7,3},{8,12},{9,13},{10,... | collective-permute-start | bytes 147464 | tf_op jit(solution)/shard_map/ppermute | solution.py:26
  49.0 3.5 %collective-permute-start.4 = (bf16[1,32,768]{2,1,0:T(8,128)(2,1)S(1)}, bf16[1,32,768]{2,1,0:T(8,128)(2,1)S(1)}, u32[]{:S(2)}, u32[]{:S(2)}) collective-permute-start(bf16[1,32,768]{2,1,0:T(8,128)(2,1)S(1)} %copy-done.13), channel_id=1, source_target_pairs={{0,5},{1,4},{2,7},{3,6},{4,1},{5,0},{6,3},{7,2},{8,13},{9,12},{10,... | collective-permute-start | bytes 147464 | tf_op jit(solution)/shard_map/ppermute | solution.py:26
  52.6 5.0 %collective-permute-start.5 = (bf16[1,32,768]{2,1,0:T(8,128)(2,1)S(1)}, bf16[1,32,768]{2,1,0:T(8,128)(2,1)S(1)}, u32[]{:S(2)}, u32[]{:S(2)}) collective-permute-start(bf16[1,32,768]{2,1,0:T(8,128)(2,1)S(1)} %copy-done.12), channel_id=1, source_target_pairs={{0,6},{1,7},{2,4},{3,5},{4,2},{5,3},{6,0},{7,1},{8,14},{9,15},{10,... | collective-permute-start | bytes 147464 | tf_op jit(solution)/shard_map/ppermute | solution.py:26
  57.6 4.4 %collective-permute-start.6 = (bf16[1,32,768]{2,1,0:T(8,128)(2,1)S(1)}, bf16[1,32,768]{2,1,0:T(8,128)(2,1)S(1)}, u32[]{:S(2)}, u32[]{:S(2)}) collective-permute-start(bf16[1,32,768]{2,1,0:T(8,128)(2,1)S(1)} %copy-done.11), channel_id=1, source_target_pairs={{0,7},{1,6},{2,5},{3,4},{4,3},{5,2},{6,1},{7,0},{8,15},{9,14},{10,... | collective-permute-start | bytes 147464 | tf_op jit(solution)/shard_map/ppermute | solution.py:26
  62.0 5.0 %collective-permute-start.7 = (bf16[1,32,768]{2,1,0:T(8,128)(2,1)S(1)}, bf16[1,32,768]{2,1,0:T(8,128)(2,1)S(1)}, u32[]{:S(2)}, u32[]{:S(2)}) collective-permute-start(bf16[1,32,768]{2,1,0:T(8,128)(2,1)S(1)} %copy-done.10), channel_id=1, source_target_pairs={{0,8},{1,9},{2,10},{3,11},{4,12},{5,13},{6,14},{7,15},{8,0},{9,1},... | collective-permute-start | bytes 147464 | tf_op jit(solution)/shard_map/ppermute | solution.py:26
  67.0 4.6 %collective-permute-start.8 = (bf16[1,32,768]{2,1,0:T(8,128)(2,1)S(1)}, bf16[1,32,768]{2,1,0:T(8,128)(2,1)S(1)}, u32[]{:S(2)}, u32[]{:S(2)}) collective-permute-start(bf16[1,32,768]{2,1,0:T(8,128)(2,1)S(1)} %copy-done.9), channel_id=1, source_target_pairs={{0,9},{1,8},{2,11},{3,10},{4,13},{5,12},{6,15},{7,14},{8,1},{9,0},... | collective-permute-start | bytes 147464 | tf_op jit(solution)/shard_map/ppermute | solution.py:26
  71.6 7.2 %collective-permute-start.9 = (bf16[1,32,768]{2,1,0:T(8,128)(2,1)S(1)}, bf16[1,32,768]{2,1,0:T(8,128)(2,1)S(1)}, u32[]{:S(2)}, u32[]{:S(2)}) collective-permute-start(bf16[1,32,768]{2,1,0:T(8,128)(2,1)S(1)} %copy-done.8), channel_id=1, source_target_pairs={{0,10},{1,11},{2,8},{3,9},{4,14},{5,15},{6,12},{7,13},{8,2},{9,3},... | collective-permute-start | bytes 147464 | tf_op jit(solution)/shard_map/ppermute | solution.py:26
  74.2 37.8 %all-to-all-start = ((bf16[16,2,12288]{2,1,0:T(2,128)(2,1)}), bf16[16,2,12288]{2,1,0:T(2,128)(2,1)S(1)}, u32[]{:S(2)}, u32[]{:S(2)}) async-start(bf16[16,2,12288]{2,1,0:T(2,128)(2,1)} %reshape.123), calls=%async_computation | async-start | bytes 1572864 | tf_op jit(solution)/shard_map/all_to_all | solution.py:51
  78.8 23.1 %collective-permute-start.10 = (bf16[1,32,768]{2,1,0:T(8,128)(2,1)S(1)}, bf16[1,32,768]{2,1,0:T(8,128)(2,1)S(1)}, u32[]{:S(2)}, u32[]{:S(2)}) collective-permute-start(bf16[1,32,768]{2,1,0:T(8,128)(2,1)S(1)} %get-tuple-element.38), channel_id=1, source_target_pairs={{0,11},{1,10},{2,9},{3,8},{4,15},{5,14},{6,13},{7,12},{8,3},{9,2},... | collective-permute-start | bytes 147464 | tf_op jit(solution)/shard_map/ppermute | solution.py:26
  119.3 4.8 %copy-start.4 = (bf16[16,32,768]{2,0,1:T(8,128)(2,1)S(1)}, bf16[16,32,768]{2,0,1:T(8,128)(2,1)}, u32[]{:S(2)}) copy-start(bf16[16,32,768]{2,0,1:T(8,128)(2,1)} %get-tuple-element.32) | copy-start | bytes 2359300
  120.4 22.3 %all-to-all-start.3 = ((bf16[16,32,768]{2,1,0:T(8,128)(2,1)}), bf16[16,32,768]{2,1,0:T(8,128)(2,1)S(1)}, u32[]{:S(2)}, u32[]{:S(2)}) async-start(bf16[16,32,768]{2,1,0:T(8,128)(2,1)} %copy.49), calls=%async_computation.3 | async-start | bytes 1572864 | tf_op jit(solution)/shard_map/all_to_all | solution.py:78
  142.7 24.1 %all-to-all-start.2 = ((bf16[16,32,768]{2,1,0:T(8,128)(2,1)}), bf16[16,32,768]{2,1,0:T(8,128)(2,1)S(1)}, u32[]{:S(2)}, u32[]{:S(2)}) async-start(bf16[16,32,768]{2,1,0:T(8,128)(2,1)} %copy.45), calls=%async_computation.2 | async-start | bytes 1572864 | tf_op jit(solution)/shard_map/all_to_all | solution.py:79
  166.8 50.0 %all-to-all-start.4 = ((bf16[16,32,768]{2,1,0:T(8,128)(2,1)}), bf16[16,32,768]{2,1,0:T(8,128)(2,1)S(1)}, u32[]{:S(2)}, u32[]{:S(2)}) async-start(bf16[16,32,768]{2,1,0:T(8,128)(2,1)} %copy.50), calls=%async_computation.4 | async-start | bytes 1572864 | tf_op jit(solution)/shard_map/all_to_all | solution.py:80
  (7 other events, 11.0 us)
